TPU v7x, 128 devices: a whole 4x4x4 slice. The times are simulated.
128 devices in a mesh: fsdp: 16 (over y, x_hi, core), seq: 8 (over x_lo, z).
Axes of the slice: x: 4 (x_hi: 2, x_lo: 2; x = x_hi * 2 + x_lo), y: 4, z: 4, core: 2. Of those that a mesh axis runs over, the one named last changes fastest.
Arguments:
- normed_input: bfloat16 [16, 2048, 3072], P('fsdp', 'seq'), may hold values from -6 to 6
- queries: bfloat16 [16, 2048, 3072], P('fsdp', 'seq'), may hold values from -96 to 96
- saved_keys: bfloat16 [16, 2048, 3072], P('fsdp', 'seq'), may hold values from -6 to 6
- saved_values: bfloat16 [16, 2048, 3072], P('fsdp', 'seq'), may hold values from -6 to 6
- attention_out: bfloat16 [16, 2048, 3072], P('fsdp', 'seq'), may hold values from -6 to 6
- output_grad: bfloat16 [16, 2048, 3072], P('fsdp', 'seq'), may hold values from -6 to 6
- output_weight: bfloat16 [3072, 3072], P('fsdp'), may hold values from -0.109375 to 0.109375
- gate_table: float32 [64, 3072], replicated, may hold values from 0.25 to 2
- timestep: int32 [16], P('fsdp'), may hold values from 0 to 63
- entry_factor: bfloat16 [3072, 64], replicated, may hold values from -0.109375 to 0.109375
- merged_factor: bfloat16 [9216, 128], replicated, may hold values from -1.5 to 1.5
- mixed_factor: bfloat16 [3072, 64], replicated, may hold values from -0.109375 to 0.109375
- result_factor: bfloat16 [3072, 128], replicated, may hold values from -0.109375 to 0.109375
Outputs:
- sketches: float32 [16, 2, 8192], P('fsdp', None, 'seq')
All inputs are finite; a program needn't handle non-finite values.
Results may differ from a plain program's by a relative error of at most 0.0056.
Values may be sent and summed in bfloat16 or wider, within the bound.
A program may use at most 128 MiB of HBM per device.

v0:
```python
import math

import jax
import jax.numpy as jnp
from jax import lax
from jax.sharding import PartitionSpec as P

HEADS = 24
HD = 128


def matmul(left, right):
    return jnp.dot(
        left.astype(jnp.float32), right.astype(jnp.float32), preferred_element_type=jnp.float32
    )


def single_head(operands):
    query_head, key_head, value_head, grad_head = operands
    seq_len = query_head.shape[0]
    head_size = query_head.shape[1]
    block_rows = min(512, seq_len)
    block_count = seq_len // block_rows
    score_scale = 1.0 / math.sqrt(head_size)
    key_wide = key_head.astype(jnp.float32)
    value_wide = value_head.astype(jnp.float32)

    def block_step(running, inputs):
        key_grad, value_grad = running
        query_block, grad_block = inputs
        scores = matmul(query_block, key_wide.T) * score_scale
        row_max = jnp.max(scores, axis=-1, keepdims=True)
        shifted = jnp.exp(scores - row_max)
        weights = shifted / jnp.sum(shifted, axis=-1, keepdims=True)
        rounded = weights.astype(jnp.bfloat16)
        value_grad = value_grad + matmul(rounded.T, grad_block)
        weight_grad = matmul(grad_block, value_wide.T)
        centre = jnp.sum(weights * weight_grad, axis=-1, keepdims=True)
        score_grad = (weights * (weight_grad - centre) * score_scale).astype(jnp.bfloat16)
        query_grad = matmul(score_grad, key_wide).astype(jnp.bfloat16)
        key_grad = key_grad + matmul(score_grad.T, query_block)
        return ((key_grad, value_grad), query_grad)

    empty_grad = jnp.zeros((seq_len, head_size), jnp.float32)
    stacked = (
        query_head.reshape(block_count, block_rows, head_size),
        grad_head.reshape(block_count, block_rows, head_size),
    )
    (key_grad, value_grad), query_grad = lax.scan(block_step, (empty_grad, empty_grad), stacked)
    return (
        query_grad.reshape(seq_len, head_size),
        key_grad.astype(jnp.bfloat16),
        value_grad.astype(jnp.bfloat16),
    )


def attend_heads(pieces):
    head_major = tuple((jnp.transpose(piece[:, 0], (1, 0, 2)) for piece in pieces))
    results = lax.map(single_head, head_major)
    return tuple((jnp.transpose(part_grad, (1, 0, 2))[:, None] for part_grad in results))


def local(
    normed_input,
    queries,
    saved_keys,
    saved_values,
    attention_out,
    output_grad,
    output_weight,
    gate_table,
    timestep,
    entry_factor,
    merged_factor,
    mixed_factor,
    result_factor,
):
    tokens_here = normed_input.shape[1]
    model_width = normed_input.shape[2]
    seq_size = lax.axis_size("seq")
    seq_len = tokens_here * seq_size
    heads_local = HEADS // seq_size
    norm_factor = 1.0 / math.sqrt(seq_len)
    selector = (
        timestep[:, None] == jnp.arange(gate_table.shape[0], dtype=jnp.int32)[None, :]
    ).astype(jnp.float32)
    gate_row = jnp.dot(selector, gate_table, precision=lax.Precision.HIGHEST)
    scaled_grad = (gate_row[0][None, :] * output_grad[0].astype(jnp.float32)).astype(jnp.bfloat16)
    mixed_left = matmul(attention_out[0], mixed_factor)
    mixed_right = matmul(scaled_grad, result_factor)
    sketch_mixed = jnp.dot(mixed_left.T, mixed_right, precision=lax.Precision.HIGHEST) * norm_factor
    entry_left = matmul(normed_input[0], entry_factor)

    def to_heads(values):
        return values[0].reshape(tokens_here, seq_size, heads_local, HD)

    summed = matmul(scaled_grad, lax.all_gather(output_weight, "fsdp", axis=0, tiled=True).T)
    attention_grad = summed.astype(jnp.bfloat16)
    grad_split = attention_grad.reshape(tokens_here, seq_size, heads_local, HD)
    head_grads = attend_heads(
        (
            lax.all_to_all(to_heads(queries), "seq", split_axis=1, concat_axis=0, tiled=True),
            lax.all_to_all(to_heads(saved_keys), "seq", split_axis=1, concat_axis=0, tiled=True),
            lax.all_to_all(to_heads(saved_values), "seq", split_axis=1, concat_axis=0, tiled=True),
            lax.all_to_all(grad_split, "seq", split_axis=1, concat_axis=0, tiled=True),
        )
    )
    token_grads = (
        lax.all_to_all(head_grads[0], "seq", split_axis=0, concat_axis=1, tiled=True),
        lax.all_to_all(head_grads[1], "seq", split_axis=0, concat_axis=1, tiled=True),
        lax.all_to_all(head_grads[2], "seq", split_axis=0, concat_axis=1, tiled=True),
    )
    merged_grad = jnp.concatenate(
        [part_grad.reshape(tokens_here, model_width) for part_grad in token_grads], axis=1
    )
    merged_right = matmul(merged_grad, merged_factor)
    sketch_merged = (
        jnp.dot(entry_left.T, merged_right, precision=lax.Precision.HIGHEST) * norm_factor
    )
    partial_sketch = jnp.stack([sketch_mixed.reshape(-1), sketch_merged.reshape(-1)])[None]
    return lax.psum_scatter(partial_sketch, "seq", scatter_dimension=2, tiled=True)


def solution(mesh):
    in_specs = (
        P("fsdp", "seq", None),
        P("fsdp", "seq", None),
        P("fsdp", "seq", None),
        P("fsdp", "seq", None),
        P("fsdp", "seq", None),
        P("fsdp", "seq", None),
        P("fsdp", None),
        P(),
        P("fsdp"),
        P(),
        P(),
        P(),
        P(),
    )
    out_specs = P("fsdp", None, "seq")
    return jax.shard_map(local, mesh=mesh, in_specs=in_specs, out_specs=out_specs, check_vma=False)
```

profile of v0, /device:TPU:1, one launch (start us, length us, event | category | flops | bytes accessed | tf_op | source)
XLA Modules:
  0.0 596.7 jit_solution(7376883028925766465)
XLA Ops:
  7.3 2.6 copy.33
  9.9 6.8 %all-to-all-start = ((bf16[256,8,3,128]{0,3,2,1:T(8,128)(2,1)}), bf16[256,8,3,128]{0,3,2,1:T(8,128)(2,1)}, u32[]{:S(2)}, u32[]{:S(2)}) async-start(bf16[256,8,3,128]{0,3,2,1:T(8,128)(2,1)} %bitcast.175), calls=%async_computation | async-start | bytes 3145728 | tf_op jit(solution)/shard_map/all_to_all | solution.py:102
  16.7 2.6 copy.37
  19.3 24.4 %all-to-all-done = bf16[256,8,3,128]{0,3,2,1:T(8,128)(2,1)} async-done(((bf16[256,8,3,128]{0,3,2,1:T(8,128)(2,1)}), bf16[256,8,3,128]{0,3,2,1:T(8,128)(2,1)}, u32[]{:S(2)}, u32[]{:S(2)}) %all-to-all-start) | async-done | bytes 1572896 | tf_op jit(solution)/shard_map/all_to_all | solution.py:102
  43.6 4.3 all-to-all-start.2
  48.7 2.7 copy.39
  51.7 12.0 %all-to-all-done.2 = bf16[256,8,3,128]{0,3,2,1:T(8,128)(2,1)} async-done(((bf16[256,8,3,128]{0,3,2,1:T(8,128)(2,1)}), bf16[256,8,3,128]{0,3,2,1:T(8,128)(2,1)}, u32[]{:S(2)}, u32[]{:S(2)}) %all-to-all-start.2) | async-done | bytes 1572896 | tf_op jit(solution)/shard_map/all_to_all | solution.py:103
  63.8 7.6 %all-to-all-start.3 = ((bf16[256,8,3,128]{0,3,2,1:T(8,128)(2,1)}), bf16[256,8,3,128]{0,3,2,1:T(8,128)(2,1)}, u32[]{:S(2)}, u32[]{:S(2)}) async-start(bf16[256,8,3,128]{0,3,2,1:T(8,128)(2,1)} %bitcast.173), calls=%async_computation.3 | async-start | bytes 3145728 | tf_op jit(solution)/shard_map/all_to_all | solution.py:104
  71.4 88.0 %all-gather.2.cloned.1.call-done = bf16[3072,3072]{1,0:T(8,128)(2,1)} async-done(((bf16[192,3072]{1,0:T(8,128)(2,1)}), bf16[3072,3072]{1,0:T(8,128)(2,1)}) %all-gather.2.cloned.1.call-update) | async-done | bytes 18874384 | tf_op jit(solution)/shard_map/all_gather | solution.py:97
  159.4 10.4 %convolution_convert_fusion.1 = bf16[256,3072]{1,0:T(8,128)(2,1)} fusion(bf16[3072,3072]{1,0:T(8,128)(2,1)} %all-gather.2.cloned.1.call-done, bf16[1,256,3072]{2,1,0:T(8,128)(2,1)} %param.22, f32[3072]{0:T(1024)S(1)} %bitcast.185), kind=kOutput, calls=%fused_computation.39 | convolution fusion | flops 4834983936 | bytes 22032384 | tf_op jit(solution)/shard_map/dot_general | solution.py:13
  169.8 2.6 copy.35
  172.4 4.5 all-to-all-start.1
  176.9 2.6 copy.34
  179.5 2.6 copy.38
  182.2 2.6 copy.40
  184.8 12.8 %all-to-all-done.1 = bf16[256,8,3,128]{0,3,2,1:T(8,128)(2,1)} async-done(((bf16[256,8,3,128]{0,3,2,1:T(8,128)(2,1)}), bf16[256,8,3,128]{0,3,2,1:T(8,128)(2,1)}, u32[]{:S(2)}, u32[]{:S(2)}) %all-to-all-start.1) | async-done | bytes 1572896 | tf_op jit(solution)/shard_map/all_to_all | solution.py:105
  197.6 2.6 copy.36
  200.2 225.7 %while.30 = (s32[]{:T(128)}, bf16[3,2048,128]{2,1,0:T(8,128)(2,1)}, bf16[3,2048,128]{2,1,0:T(8,128)(2,1)}, bf16[3,2048,128]{2,1,0:T(8,128)(2,1)}, bf16[3,2048,12...) while((s32[]{:T(128)}, bf16[3,2048,128]{2,1,0:T(8,128)(2,1)}, ...), condition=%wide.region_6.7_spmd, body=%wide.region_0.6_spmd.sunk | while | flops 1365768704 | bytes 92432848 | solution.py:59
  200.2 2.2 constant_dynamic-slice_fusion.3
  202.4 2.3 bitcast_convert_fusion.3
  204.7 66.5 %while.31 = (s32[]{:T(128)}, f32[2048,128]{1,0:T(8,128)S(1)}, f32[2048,128]{1,0:T(8,128)}, bf16[4,512,128]{2,1,0:T(8,128)(2,1)}, bf16[4,512,128]{2,1,0:T(8,128)(...) while((s32[]{:T(128)}, f32[2048,128]{1,0:T(8,128)S(1)}, ...), condition=%wide.region_5.5_spmd.clone, body=%wide.region_1.4_spmd.clone.sunk | while | flops 1365244416 | bytes 79848160 | solution.py:49
  209.4 4.6 convolution_add_fusion.5
  225.8 4.9 convolution_add_fusion.5
  242.5 4.9 convolution_add_fusion.5
  247.4 2.2 multiply_reduce_fusion.5
  259.2 4.9 convolution_add_fusion.5
  264.1 2.2 multiply_reduce_fusion.5
  275.4 2.2 constant_dynamic-slice_fusion.3
  277.7 2.3 bitcast_convert_fusion.3
  280.0 66.6 %while.31 = (s32[]{:T(128)}, f32[2048,128]{1,0:T(8,128)S(1)}, f32[2048,128]{1,0:T(8,128)}, bf16[4,512,128]{2,1,0:T(8,128)(2,1)}, bf16[4,512,128]{2,1,0:T(8,128)(...) while((s32[]{:T(128)}, f32[2048,128]{1,0:T(8,128)S(1)}, ...), condition=%wide.region_5.5_spmd.clone, body=%wide.region_1.4_spmd.clone.sunk | while | flops 1365244416 | bytes 79848160 | solution.py:49
  284.7 4.6 convolution_add_fusion.5
  301.0 4.9 convolution_add_fusion.5
  317.8 4.9 convolution_add_fusion.5
  322.7 2.2 multiply_reduce_fusion.5
  334.5 4.9 convolution_add_fusion.5
  339.4 2.2 multiply_reduce_fusion.5
  350.7 2.2 constant_dynamic-slice_fusion.3
  352.9 2.3 bitcast_convert_fusion.3
  355.2 66.6 %while.31 = (s32[]{:T(128)}, f32[2048,128]{1,0:T(8,128)S(1)}, f32[2048,128]{1,0:T(8,128)}, bf16[4,512,128]{2,1,0:T(8,128)(2,1)}, bf16[4,512,128]{2,1,0:T(8,128)(...) while((s32[]{:T(128)}, f32[2048,128]{1,0:T(8,128)S(1)}, ...), condition=%wide.region_5.5_spmd.clone, body=%wide.region_1.4_spmd.clone.sunk | while | flops 1365244416 | bytes 79848160 | solution.py:49
  359.9 4.6 convolution_add_fusion.5
  364.5 2.2 multiply_reduce_fusion.5
  376.3 4.9 convolution_add_fusion.5
  381.2 2.2 multiply_reduce_fusion.5
  393.0 4.9 convolution_add_fusion.5
  409.8 4.9 convolution_add_fusion.5
  414.7 2.2 multiply_reduce_fusion.5
  425.9 4.1 copy.57
  430.1 4.4 all-to-all-start.4
  434.4 4.2 copy.56
  438.6 22.0 %all-to-all-done.4 = bf16[2048,1,3,128]{3,2,1,0:T(4,128)(2,1)} async-done(((bf16[2048,1,3,128]{3,2,1,0:T(4,128)(2,1)}), bf16[2048,1,3,128]{3,2,1,0:T(4,128)(2,1)}, u32[]{:S(2)}, u32[]{:S(2)}) %all-to-all-start.4) | async-done | bytes 1572896 | tf_op jit(solution)/shard_map/all_to_all | solution.py:109
  460.6 4.4 all-to-all-start.5
  465.0 4.2 copy.55
  469.1 22.0 %all-to-all-done.5 = bf16[2048,1,3,128]{3,2,1,0:T(4,128)(2,1)} async-done(((bf16[2048,1,3,128]{3,2,1,0:T(4,128)(2,1)}), bf16[2048,1,3,128]{3,2,1,0:T(4,128)(2,1)}, u32[]{:S(2)}, u32[]{:S(2)}) %all-to-all-start.5) | async-done | bytes 1572896 | tf_op jit(solution)/shard_map/all_to_all | solution.py:110
  491.1 4.5 all-to-all-start.6
  501.1 3.0 copy.42
  504.1 2.6 copy.43
  506.7 3.0 copy.45
  509.8 2.6 copy.46
  512.3 9.5 %all-to-all-done.6 = bf16[2048,1,3,128]{3,2,1,0:T(4,128)(2,1)} async-done(((bf16[2048,1,3,128]{3,2,1,0:T(4,128)(2,1)}), bf16[2048,1,3,128]{3,2,1,0:T(4,128)(2,1)}, u32[]{:S(2)}, u32[]{:S(2)}) %all-to-all-start.6) | async-done | bytes 1572896 | tf_op jit(solution)/shard_map/all_to_all | solution.py:111
  521.8 3.0 copy.48
  524.8 2.6 copy.49
  527.5 3.3 fusion.20
  531.0 6.4 %copy.50 = f32[1,2,8192]{1,0,2:T(1,128)} copy(f32[1,2,8192]{2,1,0:T(2,128)S(1)} %maximum_bitcast_fusion) | data formatting | bytes 131072
  537.5 50.6 %reduce-scatter.4.cloned.1.call-done = f32[1024,2]{1,0:T(8,128)} async-done(((f32[8192,2]{1,0:T(8,128)}), f32[1024,2]{1,0:T(8,128)}) %reduce-scatter.4.cloned.1.call-update) | async-done | bytes 8208
  (215 shorter events, 146.7 us)
Async XLA Ops:
  6.5 520.9 %copy-start = (bf16[9216,128]{1,0:T(8,128)(2,1)S(1)}, bf16[9216,128]{1,0:T(8,128)(2,1)}, u32[]{:S(2)}) copy-start(bf16[9216,128]{1,0:T(8,128)(2,1)} %param.27) | copy-start | bytes 7077892
  6.5 152.8 %all-gather.2.cloned.1.call-start = ((), (), s32[]{:S(2)}) async-start(), calls=%async_computation.8 | async-start | bytes 20054016 | tf_op jit(solution)/shard_map/all_gather | solution.py:97
  9.9 33.8 %all-to-all-start = ((bf16[256,8,3,128]{0,3,2,1:T(8,128)(2,1)}), bf16[256,8,3,128]{0,3,2,1:T(8,128)(2,1)}, u32[]{:S(2)}, u32[]{:S(2)}) async-start(bf16[256,8,3,128]{0,3,2,1:T(8,128)(2,1)} %bitcast.175), calls=%async_computation | async-start | bytes 3145728 | tf_op jit(solution)/shard_map/all_to_all | solution.py:102
  43.6 20.1 %all-to-all-start.2 = ((bf16[256,8,3,128]{0,3,2,1:T(8,128)(2,1)}), bf16[256,8,3,128]{0,3,2,1:T(8,128)(2,1)}, u32[]{:S(2)}, u32[]{:S(2)}) async-start(bf16[256,8,3,128]{0,3,2,1:T(8,128)(2,1)} %bitcast.174), calls=%async_computation.2 | async-start | bytes 3145728 | tf_op jit(solution)/shard_map/all_to_all | solution.py:103
  47.9 3.4 copy-start.7
  51.7 118.1 %copy-start.10 = (f32[1,3072]{1,0:T(1,128)}, f32[1,3072]{1,0:T(1,128)S(1)}, u32[]{:S(2)}) copy-start(f32[1,3072]{1,0:T(1,128)S(1)} %fusion.34) | copy-start | bytes 36868
  63.8 108.7 %all-to-all-start.3 = ((bf16[256,8,3,128]{0,3,2,1:T(8,128)(2,1)}), bf16[256,8,3,128]{0,3,2,1:T(8,128)(2,1)}, u32[]{:S(2)}, u32[]{:S(2)}) async-start(bf16[256,8,3,128]{0,3,2,1:T(8,128)(2,1)} %bitcast.173), calls=%async_computation.3 | async-start | bytes 3145728 | tf_op jit(solution)/shard_map/all_to_all | solution.py:104
  172.4 25.2 %all-to-all-start.1 = ((bf16[256,8,3,128]{0,3,2,1:T(8,128)(2,1)}), bf16[256,8,3,128]{0,3,2,1:T(8,128)(2,1)}, u32[]{:S(2)}, u32[]{:S(2)}) async-start(bf16[256,8,3,128]{0,3,2,1:T(8,128)(2,1)} %bitcast.172), calls=%async_computation.1 | async-start | bytes 3145728 | tf_op jit(solution)/shard_map/all_to_all | solution.py:105
  206.6 1.9 copy-start.1
  209.4 4.6 copy-start.2
  209.4 4.6 copy-start.5
  217.7 2.0 copy-start.3
  223.0 1.9 copy-start.1
  225.8 4.9 copy-start.2
  225.8 4.9 copy-start.5
  234.4 2.0 copy-start.3
  239.7 1.9 copy-start.1
  242.5 4.9 copy-start.2
  242.5 4.9 copy-start.5
  251.1 2.0 copy-start.3
  256.5 1.9 copy-start.1
  259.2 4.9 copy-start.2
  259.2 4.9 copy-start.5
  267.9 2.0 copy-start.3
  281.9 1.9 copy-start.1
  284.6 4.6 copy-start.2
  284.7 4.6 copy-start.5
  293.0 2.0 copy-start.3
  298.3 1.9 copy-start.1
  301.0 4.9 copy-start.2
  301.0 4.9 copy-start.5
  309.7 2.0 copy-start.3
  315.0 1.9 copy-start.1
  317.8 4.9 copy-start.2
  317.8 4.9 copy-start.5
  326.4 2.0 copy-start.3
  331.7 1.9 copy-start.1
  334.5 4.9 copy-start.2
  334.5 4.9 copy-start.5
  343.1 2.0 copy-start.3
  357.1 1.9 copy-start.1
  359.9 4.6 copy-start.2
  359.9 4.6 copy-start.5
  368.2 2.0 copy-start.3
  373.5 1.9 copy-start.1
  376.3 4.9 copy-start.2
  376.3 4.9 copy-start.5
  384.9 2.0 copy-start.3
  390.3 1.9 copy-start.1
  393.0 4.9 copy-start.2
  393.0 4.9 copy-start.5
  401.7 2.0 copy-start.3
  407.0 1.9 copy-start.1
  409.7 4.9 copy-start.2
  409.7 4.9 copy-start.5
  418.4 2.0 copy-start.3
  430.1 30.5 %all-to-all-start.4 = ((bf16[2048,1,3,128]{3,2,1,0:T(4,128)(2,1)}), bf16[2048,1,3,128]{3,2,1,0:T(4,128)(2,1)}, u32[]{:S(2)}, u32[]{:S(2)}) async-start(bf16[2048,1,3,128]{3,2,1,0:T(4,128)(2,1)} %bitcast.171), calls=%async_computation.4 | async-start | bytes 4194304 | tf_op jit(solution)/shard_map/all_to_all | solution.py:109
  460.6 30.5 %all-to-all-start.5 = ((bf16[2048,1,3,128]{3,2,1,0:T(4,128)(2,1)}), bf16[2048,1,3,128]{3,2,1,0:T(4,128)(2,1)}, u32[]{:S(2)}, u32[]{:S(2)}) async-start(bf16[2048,1,3,128]{3,2,1,0:T(4,128)(2,1)} %bitcast.170), calls=%async_computation.5 | async-start | bytes 4194304 | tf_op jit(solution)/shard_map/all_to_all | solution.py:110
  491.1 4.8 copy-start.8
  491.1 6.9 %copy-start.11 = (f32[1,3072]{1,0:T(1,128)S(1)}, f32[1,3072]{1,0:T(1,128)}, u32[]{:S(2)}) copy-start(f32[1,3072]{1,0:T(1,128)} %copy-done.10) | copy-start | bytes 36868
  491.1 30.6 %all-to-all-start.6 = ((bf16[2048,1,3,128]{3,2,1,0:T(4,128)(2,1)}), bf16[2048,1,3,128]{3,2,1,0:T(4,128)(2,1)}, u32[]{:S(2)}, u32[]{:S(2)}) async-start(bf16[2048,1,3,128]{3,2,1,0:T(4,128)(2,1)} %bitcast.169), calls=%async_computation.6 | async-start | bytes 4194304 | tf_op jit(solution)/shard_map/all_to_all | solution.py:111
  495.6 4.8 copy-start.9
  495.6 92.5 %reduce-scatter.4.cloned.1.call-start = ((), (), s32[]{:S(2)}) async-start(), calls=%async_computation.9 | async-start | bytes 4718592
  495.9 4.6 copy-start.6
  (3 other events, 4.2 us)
Sparse Core Ops, SparseCore 0:
  9.8 149.5 all-gather.1
  537.6 50.4 reduce-scatter.3
where the time goes:
time: 599 us; the launch traced here: 597 us
  waiting for transfers between devices  242 us (40%)
  matrix products  167 us (28%)
  local copies, waits for them, and re-layouts  103 us (17%)
  starting transfers between devices  36.7 us (6%)
  other arithmetic  33.1 us (6%)
  between operations  14.3 us (2%)
    dot_general x65, matrix products, matmul(): jnp.dot(left.astype(jnp.float32), right.astype(jnp.float32), preferred_el...  166 us
    all_gather x1, waiting for transfers between devices, local(): lax.all_gather(output_weight, 'fsdp', axis=0, tiled=True)  88 us
    unnamed x3, waiting for transfers between devices  51.4 us
    while x102, local copies, waits for them, and re-layouts  25 us
    all_to_all x1, waiting for transfers between devices, local(): lax.all_to_all(to_heads(queries), 'seq', split_axis=1, concat_axis=0, til...  24.4 us
    all_to_all x1, waiting for transfers between devices, local(): lax.all_to_all(head_grads[0], 'seq', split_axis=0, concat_axis=1, tiled=T...  22 us
    all_to_all x1, waiting for transfers between devices, local(): lax.all_to_all(head_grads[1], 'seq', split_axis=0, concat_axis=1, tiled=T...  22 us
    convert_element_type x12, other arithmetic, block_step(): (weights * (weight_grad - centre) * score_scale).astype(jnp.bfloat16)  18.1 us
  transfers between devices with their start and end apart: 9, of which 8 were waited for; matrix products, arithmetic and copies ran while one was open for 9% of the time, Pallas kernels for 0%

commit v1 on v0

v1 whole, which is shorter than its diff:
```python
import math

import jax
import jax.numpy as jnp
from jax import lax
from jax.experimental import pallas as pl
from jax.experimental.pallas import tpu as pltpu
from jax.sharding import PartitionSpec as P

F32 = jnp.float32
BF16 = jnp.bfloat16
MESH = pl.DeviceIdType.MESH

D = 3072
HD = 128
TOK = 256
SEQ = 2048
PEERS = 8
HPD = 3
RIN = 64
ROUT = 128
WROWS = 192
HALF = 96
RINGS = 4
SCALE = 1.0 / math.sqrt(HD)
EXP2_SCALE = SCALE * math.log2(math.e)
NORM = 1.0 / math.sqrt(SEQ)
QB = 512
KB = 256

NN = (((1,), (0,)), ((), ()))
NT = (((1,), (1,)), ((), ()))
TN = (((0,), (0,)), ((), ()))


def dot(left, right, dims=NN, precision=None):
    return lax.dot_general(left, right, dims, precision=precision, preferred_element_type=F32)


def split(values):
    high = values.astype(BF16)
    return high, (values - high.astype(F32)).astype(BF16)


def dot_split(values, right, dims=NN):
    high, low = split(values)
    return dot(high, right, dims) + dot(low, right, dims)


def fold(values, reduce):
    rows, columns = values.shape
    return reduce(values.reshape(rows // 8, 8, columns), axis=0)


def attend_block(start, first, head, qb, kb_ref, vb, gt, et, s_ref, p_ref, dp_ref, accv, acck):
    q_rows = pl.ds(start, QB)
    qf = qb[head, q_rows, :].astype(F32).T
    q_both = jnp.concatenate(split(qf * EXP2_SCALE), 0)
    steps = SEQ // KB
    top = None
    for step in range(steps):
        rows = pl.ds(step * KB, KB)
        keys = kb_ref[head, rows, :]
        scores = dot(jnp.concatenate([keys, keys], 1), q_both)
        s_ref[rows, :] = scores
        part = fold(scores, jnp.max)
        top = part if top is None else jnp.maximum(top, part)
    top = jnp.max(top, axis=0, keepdims=True)
    grads = gt[pl.ds(pl.multiple_of(head * HD, HD), HD), q_rows]
    total, centre = None, None
    for step in range(steps):
        rows = pl.ds(step * KB, KB)
        probs = jnp.exp2(s_ref[rows, :] - top)
        prob_grad = dot(vb[head, rows, :], grads)
        part_total = fold(probs, jnp.sum)
        part_centre = fold(probs * prob_grad, jnp.sum)
        total = part_total if total is None else total + part_total
        centre = part_centre if centre is None else centre + part_centre
        p_ref[rows, :] = probs.astype(BF16)
        dp_ref[rows, :] = prob_grad
    inverse = 1.0 / jnp.sum(total, axis=0, keepdims=True)
    centre = jnp.sum(centre, axis=0, keepdims=True) * inverse
    grads_scaled = (grads.astype(F32) * inverse).astype(BF16)
    inverse = inverse * SCALE
    entry_high, entry_low = split(et[:, q_rows] * inverse)
    q_entry = jnp.concatenate([(qf * inverse).astype(BF16), entry_high, entry_low], 0)
    for step in range(steps):
        rows = pl.ds(step * KB, KB)
        probs = p_ref[rows, :]
        score_grad = (probs.astype(F32) * (dp_ref[rows, :] - centre)).astype(BF16)
        add_v = dot(probs, grads_scaled, NT)
        add_k = dot(score_grad, q_entry, NT)
        if first:
            accv[rows, :] = add_v
            acck[rows, :] = add_k
        else:
            accv[rows, :] += add_v
            acck[rows, :] += add_k


def kernel(
    xn, qh, kh, vh, ao, og, wh, gates, step_ref, ef, mergedf, mixf, resf,
    out,
    qb, kb_ref, vb, gt, et, sg, wb, gst, xv, av, gv, efv, mfv, rfv, fv,
    s_ref, p_ref, dp_ref, accv, acck, part, gather,
    load_sem, qkv_recv, qkv_send, w_recv, w_send, sg_recv, sg_send,
    g_recv, g_send, e_recv, e_send, r_recv, r_send,
):
    f = lax.axis_index("fsdp")
    s = lax.axis_index("seq")
    y = f // 4
    hi = (f // 2) % 2
    core = f % 2
    lo = s // 4
    zz = s % 4
    s_across = (1 - lo) * 4 + zz
    mate = (f + 1 - 2 * core, s)
    across_f = y * 4 + (1 - hi) * 2 + core
    across = (across_f, s_across)
    up = ((f + 4) % 16, s)
    down = ((f + 12) % 16, s)

    barrier = pltpu.get_barrier_semaphore()

    @pl.loop(1, 32)
    def _(step):
        target = (y * 4 + (f % 4 + step // 8) % 4, (s + step) % 8)
        pl.semaphore_signal(barrier, inc=1, device_id=target, device_id_type=MESH)

    for target in (up, down):
        pl.semaphore_signal(barrier, inc=1, device_id=target, device_id_type=MESH)

    loads = []

    def load(source, target):
        copy = pltpu.make_async_copy(source, target, load_sem.at[len(loads)])
        copy.start()
        loads.append(copy)
        return copy

    load_og = load(og.at[0], sg.at[0])
    load_gate = load(gates, gv)
    load_w = load(wh, wb.at[y])
    load_xn = load(xn.at[0], xv)
    load_ef = load(ef, efv)
    load_ao = load(ao.at[0], av)
    load_mf = load(mixf, mfv)
    load_rf = load(resf, rfv)
    load_f = [
        load(mergedf.at[pl.ds(pl.multiple_of(kind * D + s * 384, 128), 384), :], fv.at[kind])
        for kind in range(3)
    ]

    sources = (qh, kh, vh)
    targets = (qb, kb_ref, vb)
    here = pl.ds(pl.multiple_of(s * TOK, TOK), TOK)
    for head in range(HPD):
        for which in range(3):
            columns = pl.ds(pl.multiple_of(s * 384 + head * HD, HD), HD)
            pltpu.make_async_copy(
                sources[which].at[0, :, columns],
                targets[which].at[head, here, :],
                qkv_recv.at[which, head],
            ).start()

    load_og.wait()
    load_gate.wait()
    gate = gv[pl.ds(step_ref[0], 1), :]
    for row in range(0, TOK, 32):
        rows = pl.ds(row, 32)
        sg[0, rows, :] = (gate * sg[0, rows, :].astype(F32)).astype(BF16)

    pl.semaphore_wait(barrier, 33)

    def remote(source, target, send, recv, device):
        return pltpu.make_async_remote_copy(
            src_ref=source, dst_ref=target, send_sem=send, recv_sem=recv,
            device_id=device, device_id_type=MESH,
        )

    first_half = pl.ds(0, HALF)
    second_half = pl.ds(HALF, HALF)
    w_copies = [
        remote(wh.at[first_half], wb.at[y, first_half], w_send.at[0], w_recv.at[0], up),
        remote(wh.at[second_half], wb.at[y, second_half], w_send.at[1], w_recv.at[1], down),
        remote(wh.at[second_half], wb.at[y, second_half], w_send.at[2], w_recv.at[2], up),
        remote(wh.at[first_half], wb.at[y, first_half], w_send.at[3], w_recv.at[3], down),
    ]
    for copy in w_copies:
        copy.start()
    sg_across = remote(sg.at[0], sg.at[2], sg_send.at[1], sg_recv.at[1], across)
    sg_across.start()
    sg_mate = remote(sg.at[0], sg.at[1], sg_send.at[0], sg_recv.at[0], mate)
    sg_mate.start()

    for head in range(HPD):

        @pl.loop(1, PEERS)
        def _(step):
            peer = (s + step) % PEERS
            columns = pl.ds(pl.multiple_of(peer * 384 + head * HD, HD), HD)
            for which in range(3):
                remote(
                    sources[which].at[0, :, columns],
                    targets[which].at[head, here, :],
                    qkv_send.at[which, head],
                    qkv_recv.at[which, head],
                    (f, peer),
                ).start()

    load_xn.wait()
    load_ef.wait()
    entry = dot(xv[...], efv[...])
    et[:, here] = jnp.concatenate([entry, entry], 1).T[:RIN]

    @pl.loop(1, PEERS)
    def _(step):
        peer = (s + step) % PEERS
        remote(et.at[:, here], et.at[:, here], e_send, e_recv, (f, peer)).start()

    load_ao.wait()
    load_mf.wait()
    load_rf.wait()
    mixed_left = dot(av[...], mfv[...])
    mixed_left = jnp.concatenate([mixed_left, mixed_left], 1).T[:RIN]
    mixed_right = dot(sg[0], rfv[...])
    part[0] = dot(mixed_left, mixed_right, precision=lax.Precision.HIGHEST) * NORM

    def g_copies(chunk, image):
        token_block = s if image < 2 else s_across
        image_f = (f, mate[0], across_f, across_f + 1 - 2 * core)[image]
        peer = 2 * chunk + hi
        columns = pl.ds(pl.multiple_of(token_block * TOK, TOK), TOK)
        target = gt.at[pl.ds(pl.multiple_of(core * WROWS, WROWS), WROWS), columns]
        slot = chunk * 4 + image
        far = remote(
            gst.at[chunk, image], target, g_send.at[slot], g_recv, (image_f, peer)
        )
        near = pltpu.make_async_copy(gst.at[chunk, image], target, g_recv)
        return far, near, peer

    def make_g(chunk, image):
        gst[chunk, image] = dot(wb[chunk], sg[image], NT).astype(BF16)
        far, near, peer = g_copies(chunk, image)
        if image == 0:

            @pl.when(peer == s)
            def _():
                near.start()

            @pl.when(peer != s)
            def _():
                far.start()
        else:
            far.start()

    below, above, opposite = (y + 3) % 4, (y + 1) % 4, (y + 2) % 4
    load_w.wait()
    make_g(y, 0)
    sg_mate.wait_recv()
    make_g(y, 1)
    w_copies[0].wait_recv()
    relay_up = remote(
        wb.at[below, first_half], wb.at[below, first_half], w_send.at[4], w_recv.at[4], up
    )
    relay_up.start()
    w_copies[1].wait_recv()
    relay_down = remote(
        wb.at[above, second_half], wb.at[above, second_half], w_send.at[5], w_recv.at[5], down
    )
    relay_down.start()
    w_copies[2].wait_recv()
    w_copies[3].wait_recv()

    def two(image):
        @pl.loop(0, 2)
        def _(step):
            make_g((y + 1 + 2 * step) % 4, image)

    def four(image):
        @pl.loop(0, 4)
        def _(step):
            make_g((y + step) % 4, image)

    two(0)
    two(1)
    sg_across.wait_recv()
    sg_pass = remote(sg.at[2], sg.at[3], sg_send.at[2], sg_recv.at[2], mate)
    sg_pass.start()
    relay_up.wait_recv()
    relay_down.wait_recv()
    make_g(opposite, 0)
    make_g(opposite, 1)
    four(2)
    sg_pass.wait_recv()
    four(3)

    for copy in load_f:
        copy.wait()
    rest = pl.ds(0, SEQ - TOK)
    pltpu.make_async_copy(et.at[:, rest], et.at[:, rest], e_recv).wait()
    pltpu.make_async_copy(gt, gt, g_recv).wait()
    part[1] = jnp.zeros((RIN, ROUT), F32)

    @pl.loop(0, HPD)
    def _(head):
        for which in range(3):
            whole = targets[which].at[head]
            pltpu.make_async_copy(whole, whole, qkv_recv.at[which, head]).wait()
        refs = (qb, kb_ref, vb, gt, et, s_ref, p_ref, dp_ref, accv, acck)
        attend_block(0, True, head, *refs)

        @pl.loop(1, SEQ // QB)
        def _(block):
            attend_block(pl.multiple_of(block * QB, QB), False, head, *refs)

        entry_both = jnp.concatenate(split(et[...]), 0)
        value_part = dot(entry_both, accv[...].astype(BF16))
        key_part = dot(entry_both, acck[:, :HD].astype(BF16))
        query_part = dot_split(acck[:, HD:], kb_ref[head], TN)
        columns = pl.ds(pl.multiple_of(head * HD, HD), HD)
        sketch = None
        for kind, piece in enumerate((query_part, key_part, value_part)):
            term = dot_split(piece[:RIN] + piece[RIN:], fv[kind, columns, :])
            sketch = term if sketch is None else sketch + term
        part[1] += sketch * NORM

    @pl.loop(1, PEERS)
    def _(step):
        peer = (s + step) % PEERS
        rows = pl.ds(pl.multiple_of(peer * 8, 8), 8)
        remote(part.at[:, rows, :], gather.at[s], r_send, r_recv, (f, peer)).start()

    gather[s] = part[:, pl.ds(pl.multiple_of(s * 8, 8), 8), :]
    seven = gather.at[pl.ds(0, PEERS - 1)]
    pltpu.make_async_copy(seven, seven, r_recv).wait()
    summed = jnp.sum(gather[...], axis=0)
    for sketch in range(2):
        for row in range(8):
            out[0, sketch : sketch + 1, row * 128 : (row + 1) * 128] = summed[
                sketch, row : row + 1, :
            ]

    pltpu.make_async_copy(seven, seven, r_send).wait()
    pltpu.make_async_copy(et.at[:, rest], et.at[:, rest], e_send).wait()
    for head in range(HPD):
        for which in range(3):
            sent = targets[which].at[head, rest]
            pltpu.make_async_copy(sent, sent, qkv_send.at[which, head]).wait()
    for copy in w_copies + [relay_up, relay_down]:
        copy.wait_send()
    for copy in (sg_mate, sg_across, sg_pass):
        copy.wait_send()
    for image in range(4):

        @pl.loop(0, RINGS)
        def _(chunk):
            far, _, peer = g_copies(chunk, image)
            if image == 0:

                @pl.when(peer != s)
                def _():
                    far.wait_send()
            else:
                far.wait_send()


def local(*operands):
    dma = pltpu.SemaphoreType.DMA
    any_spec = pl.BlockSpec(memory_space=pl.ANY)
    in_specs = [any_spec] * 13
    in_specs[8] = pl.BlockSpec(memory_space=pltpu.SMEM)
    return pl.pallas_call(
        kernel,
        out_shape=jax.ShapeDtypeStruct((1, 2, RIN * ROUT // PEERS), F32),
        in_specs=in_specs,
        out_specs=pl.BlockSpec(memory_space=pltpu.VMEM),
        scratch_shapes=[
            pltpu.VMEM((HPD, SEQ, HD), BF16),
            pltpu.VMEM((HPD, SEQ, HD), BF16),
            pltpu.VMEM((HPD, SEQ, HD), BF16),
            pltpu.VMEM((HPD * HD, SEQ), BF16),
            pltpu.VMEM((RIN, SEQ), F32),
            pltpu.VMEM((4, TOK, D), BF16),
            pltpu.VMEM((RINGS, WROWS, D), BF16),
            pltpu.VMEM((RINGS, 4, WROWS, TOK), BF16),
            pltpu.VMEM((TOK, D), BF16),
            pltpu.VMEM((TOK, D), BF16),
            pltpu.VMEM((64, D), F32),
            pltpu.VMEM((D, RIN), BF16),
            pltpu.VMEM((D, RIN), BF16),
            pltpu.VMEM((D, ROUT), BF16),
            pltpu.VMEM((3, HPD * HD, ROUT), BF16),
            pltpu.VMEM((SEQ, QB), F32),
            pltpu.VMEM((SEQ, QB), BF16),
            pltpu.VMEM((SEQ, QB), F32),
            pltpu.VMEM((SEQ, HD), F32),
            pltpu.VMEM((SEQ, 2 * HD), F32),
            pltpu.VMEM((2, RIN, ROUT), F32),
            pltpu.VMEM((PEERS, 2, 8, ROUT), F32),
            dma((11,)),
            dma((3, HPD)),
            dma((3, HPD)),
            dma((6,)),
            dma((6,)),
            dma((3,)),
            dma((3,)),
            dma,
            dma((16,)),
            dma,
            dma,
            dma,
            dma,
        ],
        compiler_params=pltpu.CompilerParams(
            collective_id=0, has_side_effects=True, vmem_limit_bytes=60 << 20
        ),
        cost_estimate=pl.CostEstimate(
            flops=26 * 10**9, bytes_accessed=16 * 2**20, transcendentals=13 * 10**6
        ),
    )(*operands)


def solution(mesh):
    in_specs = (
        P("fsdp", "seq", None),
        P("fsdp", "seq", None),
        P("fsdp", "seq", None),
        P("fsdp", "seq", None),
        P("fsdp", "seq", None),
        P("fsdp", "seq", None),
        P("fsdp", None),
        P(),
        P("fsdp"),
        P(),
        P(),
        P(),
        P(),
    )
    out_specs = P("fsdp", None, "seq")
    return jax.shard_map(local, mesh=mesh, in_specs=in_specs, out_specs=out_specs, check_vma=False)
```

time: 599 us -> 160 us (0.27)
  waiting for transfers between devices: 242 us -> 0 us
  matrix products: 167 us -> 0 us
  Pallas kernels: 0 us -> 154 us
  local copies, waits for them, and re-layouts: 103 us -> 5.62 us
  starting transfers between devices: 36.7 us -> 0 us
  other arithmetic: 33.1 us -> 0 us
  between operations: 14.3 us -> 0.66 us
    dot_general x68 -> x0, matrix products: 167 us -> none  [the longest x65 166 us: matmul(): jnp.dot(left.astype(jnp.float32), right.astype(jnp.float32), preferred_el...]
    pallas_call x0 -> x1, Pallas kernels: none -> 154 us  [local(): pl.pallas_call(kernel, out_shape=jax.ShapeDtypeStruct((1, 2, RIN * ROUT /...]
    all_to_all x7 -> x0, waiting for transfers between devices: 103 us -> none  [the longest x1 24.4 us: local(): lax.all_to_all(to_heads(queries), 'seq', split_axis=1, concat_axis=0, til...]
    all_gather x1 -> x0, waiting for transfers between devices: 88 us -> none  [local(): lax.all_gather(output_weight, 'fsdp', axis=0, tiled=True)]
    unnamed x3 -> x0, waiting for transfers between devices: 51.4 us -> none
    while x105 -> x0, local copies, waits for them, and re-layouts: 37.5 us -> none
    all_to_all x7 -> x0, starting transfers between devices: 36.4 us -> none  [the longest x1 7.63 us: local(): lax.all_to_all(to_heads(saved_values), 'seq', split_axis=1, concat_axis=0...]
    all_to_all x10 -> x0, local copies, waits for them, and re-layouts: 27.3 us -> none  [the longest x2 5.67 us: local(): lax.all_to_all(head_grads[2], 'seq', split_axis=0, concat_axis=1, tiled=T...]
  transfers between devices with their start and end apart: 9 -> 0, of which waited for: 8 -> 0; matrix products, arithmetic and copies ran while one was open for 9% -> 0% of each run, Pallas kernels for 0% -> 0%
where the time goes in v1:
time: 160 us
  Pallas kernels  154 us (96%)
  local copies, waits for them, and re-layouts  5.62 us (4%)
    pallas_call x1, Pallas kernels, local(): pl.pallas_call(kernel, out_shape=jax.ShapeDtypeStruct((1, 2, RIN * ROUT /...  154 us
    unnamed x3, local copies, waits for them, and re-layouts  5.62 us

profile of v1, /device:TPU:1, one launch (start us, length us, event | category | flops | bytes accessed | tf_op | source)
XLA Modules:
  0.0 160.2 jit_solution(15685322983716842472)
XLA Ops:
  0.7 2.2 %copy.14.ef = bf16[3072,64]{1,0:T(8,128)(2,1)} copy(bf16[3072,64]{0,1:T(8,128)(2,1)} %param.22) | data formatting | bytes 786432 | tf_op args[9]
  2.8 2.2 %copy.15.mixf = bf16[3072,64]{1,0:T(8,128)(2,1)} copy(bf16[3072,64]{0,1:T(8,128)(2,1)} %param.24) | data formatting | bytes 786432 | tf_op args[11]
  5.0 153.9 %shard_map.127 = f32[1,2,1024]{2,1,0:T(2,128)} custom-call(bf16[1,256,3072]{2,1,0:T(8,128)(2,1)} %xn.1, bf16[1,256,3072]{2,1,0:T(8,128)(2,1)} %qh.1, bf16[1,256,3072]{2,1,0:T(8,128)(2,1)} %kh.1, bf16[1,256,3072]{2,1,0:T(8,128)(2,1)} %vh.1, bf16[1,256,3072]{2,1,0:T(8,128)(2,1)} %ao.1, bf16[1,256,3072]{2,1,0:T(8,128)(2,1)} %og.1, bf16[192,3072]{1,0:T(8,128)(2,1)} %wh.1, ...), custom_call_target="tpu_custom_call" | custom-call | flops 25999998976 | bytes 16777216 | tf_op jit(solution)/shard_map/pallas_call | solution.py:373
  158.9 1.3 copy.18

commit v2 on v1

--- a/solution.py
+++ b/solution.py
@@ -25,8 +25,10 @@
 SCALE = 1.0 / math.sqrt(HD)
 EXP2_SCALE = SCALE * math.log2(math.e)
 NORM = 1.0 / math.sqrt(SEQ)
-QB = 512
+SB = 256
+GB = 1024
 KB = 256
+KEY_STEPS = SEQ // KB
 
 NN = (((1,), (0,)), ((), ()))
 NT = (((1,), (1,)), ((), ()))
@@ -52,42 +54,82 @@
     return reduce(values.reshape(rows // 8, 8, columns), axis=0)
 
 
-def attend_block(start, first, head, qb, kb_ref, vb, gt, et, s_ref, p_ref, dp_ref, accv, acck):
-    q_rows = pl.ds(start, QB)
-    qf = qb[head, q_rows, :].astype(F32).T
-    q_both = jnp.concatenate(split(qf * EXP2_SCALE), 0)
-    steps = SEQ // KB
-    top = None
-    for step in range(steps):
+def softmax_head(head, slot, qb, kb_ref, vb, s_ref, p_ref, l_ref, o_ref, vt):
+    vt[...] = vb[head].T
+
+    def queries(start):
+        wide = qb[head, pl.ds(start, SB), :].astype(F32).T
+        return jnp.concatenate(split(wide * EXP2_SCALE), 0)
+
+    def score(both, side, step, top):
         rows = pl.ds(step * KB, KB)
         keys = kb_ref[head, rows, :]
-        scores = dot(jnp.concatenate([keys, keys], 1), q_both)
-        s_ref[rows, :] = scores
+        scores = dot(jnp.concatenate([keys, keys], 1), both)
+        s_ref[side, rows, :] = scores
         part = fold(scores, jnp.max)
-        top = part if top is None else jnp.maximum(top, part)
-    top = jnp.max(top, axis=0, keepdims=True)
-    grads = gt[pl.ds(pl.multiple_of(head * HD, HD), HD), q_rows]
-    total, centre = None, None
-    for step in range(steps):
+        return part if top is None else jnp.maximum(top, part)
+
+    def exponential(columns, side, step, top, total, mixed):
         rows = pl.ds(step * KB, KB)
-        probs = jnp.exp2(s_ref[rows, :] - top)
+        probs = jnp.exp2(s_ref[side, rows, :] - top)
+        part = fold(probs, jnp.sum)
+        probs = probs.astype(BF16)
+        p_ref[slot, rows, columns] = probs
+        piece = dot(vt[:, rows], probs)
+        if total is None:
+            return part, piece
+        return total + part, mixed + piece
+
+    def finish(columns, total, mixed):
+        l_ref[pl.ds(slot, 1), columns] = jnp.sum(total, axis=0, keepdims=True)
+        o_ref[slot, :, columns] = mixed
+
+    def highest(top):
+        return jnp.max(top, axis=0, keepdims=True)
+
+    def stage(block, side, top):
+        columns = pl.ds(pl.multiple_of(block * SB, SB), SB)
+        both = queries(pl.multiple_of((block + 1) * SB, SB))
+        later, total, mixed = None, None, None
+        for step in range(KEY_STEPS):
+            later = score(both, 1 - side, step, later)
+            total, mixed = exponential(columns, side, step, top, total, mixed)
+        finish(columns, total, mixed)
+        return highest(later)
+
+    both, top = queries(0), None
+    for step in range(KEY_STEPS):
+        top = score(both, 0, step, top)
+    blocks = SEQ // SB
+
+    def pair(index, top):
+        return stage(2 * index + 1, 1, stage(2 * index, 0, top))
+
+    top = lax.fori_loop(0, blocks // 2 - 1, pair, highest(top))
+    top = stage(blocks - 2, 0, top)
+    columns = pl.ds(SEQ - SB, SB)
+    total, mixed = None, None
+    for step in range(KEY_STEPS):
+        total, mixed = exponential(columns, 1, step, top, total, mixed)
+    finish(columns, total, mixed)
+
+
+def gradient_block(start, first, head, slot, qb, vb, gt, et, p_ref, l_ref, o_ref, accv, acck):
+    columns = pl.ds(start, GB)
+    inverse = 1.0 / l_ref[pl.ds(slot, 1), columns]
+    grads = gt[pl.ds(pl.multiple_of(head * HD, HD), HD), columns]
+    wide = grads.astype(F32)
+    centre = jnp.sum(wide * o_ref[slot, :, columns], axis=0, keepdims=True) * inverse
+    grads_scaled = (wide * inverse).astype(BF16)
+    inverse = inverse * SCALE
+    entry_high, entry_low = split(et[:, columns].astype(F32) * inverse)
+    q_scaled = (qb[head, columns, :].astype(F32).T * inverse).astype(BF16)
+    q_entry = jnp.concatenate([q_scaled, entry_high, entry_low], 0)
+    for step in range(KEY_STEPS):
+        rows = pl.ds(step * KB, KB)
+        probs = p_ref[slot, rows, columns]
         prob_grad = dot(vb[head, rows, :], grads)
-        part_total = fold(probs, jnp.sum)
-        part_centre = fold(probs * prob_grad, jnp.sum)
-        total = part_total if total is None else total + part_total
-        centre = part_centre if centre is None else centre + part_centre
-        p_ref[rows, :] = probs.astype(BF16)
-        dp_ref[rows, :] = prob_grad
-    inverse = 1.0 / jnp.sum(total, axis=0, keepdims=True)
-    centre = jnp.sum(centre, axis=0, keepdims=True) * inverse
-    grads_scaled = (grads.astype(F32) * inverse).astype(BF16)
-    inverse = inverse * SCALE
-    entry_high, entry_low = split(et[:, q_rows] * inverse)
-    q_entry = jnp.concatenate([(qf * inverse).astype(BF16), entry_high, entry_low], 0)
-    for step in range(steps):
-        rows = pl.ds(step * KB, KB)
-        probs = p_ref[rows, :]
-        score_grad = (probs.astype(F32) * (dp_ref[rows, :] - centre)).astype(BF16)
+        score_grad = (probs.astype(F32) * (prob_grad - centre)).astype(BF16)
         add_v = dot(probs, grads_scaled, NT)
         add_k = dot(score_grad, q_entry, NT)
         if first:
@@ -102,7 +144,7 @@
     xn, qh, kh, vh, ao, og, wh, gates, step_ref, ef, mergedf, mixf, resf,
     out,
     qb, kb_ref, vb, gt, et, sg, wb, gst, xv, av, gv, efv, mfv, rfv, fv,
-    s_ref, p_ref, dp_ref, accv, acck, part, gather,
+    s_ref, p_ref, l_ref, o_ref, vt, accv, acck, part, gather,
     load_sem, qkv_recv, qkv_send, w_recv, w_send, sg_recv, sg_send,
     g_recv, g_send, e_recv, e_send, r_recv, r_send,
 ):
@@ -163,13 +205,6 @@
                 qkv_recv.at[which, head],
             ).start()
 
-    load_og.wait()
-    load_gate.wait()
-    gate = gv[pl.ds(step_ref[0], 1), :]
-    for row in range(0, TOK, 32):
-        rows = pl.ds(row, 32)
-        sg[0, rows, :] = (gate * sg[0, rows, :].astype(F32)).astype(BF16)
-
     pl.semaphore_wait(barrier, 33)
 
     def remote(source, target, send, recv, device):
@@ -188,16 +223,13 @@
     ]
     for copy in w_copies:
         copy.start()
-    sg_across = remote(sg.at[0], sg.at[2], sg_send.at[1], sg_recv.at[1], across)
-    sg_across.start()
-    sg_mate = remote(sg.at[0], sg.at[1], sg_send.at[0], sg_recv.at[0], mate)
-    sg_mate.start()
-
-    for head in range(HPD):
-
+    def peer_of(step):
+        return ((lo + step // 4) % 2) * 4 + (zz + step) % 4
+
+    def send_head(head):
         @pl.loop(1, PEERS)
         def _(step):
-            peer = (s + step) % PEERS
+            peer = peer_of(step)
             columns = pl.ds(pl.multiple_of(peer * 384 + head * HD, HD), HD)
             for which in range(3):
                 remote(
@@ -208,21 +240,35 @@
                     (f, peer),
                 ).start()
 
+    send_head(0)
+
+    load_og.wait()
+    load_gate.wait()
+    gate = gv[pl.ds(step_ref[0], 1), :]
+    for row in range(0, TOK, 32):
+        rows = pl.ds(row, 32)
+        sg[0, rows, :] = (gate * sg[0, rows, :].astype(F32)).astype(BF16)
+
+    sg_across = remote(sg.at[0], sg.at[2], sg_send.at[1], sg_recv.at[1], across)
+    sg_across.start()
+    sg_mate = remote(sg.at[0], sg.at[1], sg_send.at[0], sg_recv.at[0], mate)
+    sg_mate.start()
+
+    send_head(1)
+
     load_xn.wait()
     load_ef.wait()
-    entry = dot(xv[...], efv[...])
-    et[:, here] = jnp.concatenate([entry, entry], 1).T[:RIN]
+    et[:, here] = dot(efv[...], xv[...], NT).astype(BF16)
 
     @pl.loop(1, PEERS)
     def _(step):
-        peer = (s + step) % PEERS
+        peer = peer_of(step)
         remote(et.at[:, here], et.at[:, here], e_send, e_recv, (f, peer)).start()
 
     load_ao.wait()
     load_mf.wait()
     load_rf.wait()
-    mixed_left = dot(av[...], mfv[...])
-    mixed_left = jnp.concatenate([mixed_left, mixed_left], 1).T[:RIN]
+    mixed_left = dot(mfv[...], av[...], NT)
     mixed_right = dot(sg[0], rfv[...])
     part[0] = dot(mixed_left, mixed_right, precision=lax.Precision.HIGHEST) * NORM
 
@@ -269,6 +315,17 @@
         wb.at[above, second_half], wb.at[above, second_half], w_send.at[5], w_recv.at[5], down
     )
     relay_down.start()
+
+    def wait_head(head):
+        for which in range(3):
+            whole = targets[which].at[head]
+            pltpu.make_async_copy(whole, whole, qkv_recv.at[which, head]).wait()
+
+    def softmax_of(head, slot):
+        softmax_head(head, slot, qb, kb_ref, vb, s_ref, p_ref, l_ref, o_ref, vt)
+
+    wait_head(0)
+    softmax_of(0, 0)
     w_copies[2].wait_recv()
     w_copies[3].wait_recv()
 
@@ -287,13 +344,18 @@
     sg_across.wait_recv()
     sg_pass = remote(sg.at[2], sg.at[3], sg_send.at[2], sg_recv.at[2], mate)
     sg_pass.start()
+    make_g(y, 2)
+    two(2)
     relay_up.wait_recv()
     relay_down.wait_recv()
     make_g(opposite, 0)
     make_g(opposite, 1)
-    four(2)
+    make_g(opposite, 2)
     sg_pass.wait_recv()
     four(3)
+    send_head(2)
+    wait_head(1)
+    softmax_of(1, 1)
 
     for copy in load_f:
         copy.wait()
@@ -302,32 +364,37 @@
     pltpu.make_async_copy(gt, gt, g_recv).wait()
     part[1] = jnp.zeros((RIN, ROUT), F32)
 
-    @pl.loop(0, HPD)
-    def _(head):
-        for which in range(3):
-            whole = targets[which].at[head]
-            pltpu.make_async_copy(whole, whole, qkv_recv.at[which, head]).wait()
-        refs = (qb, kb_ref, vb, gt, et, s_ref, p_ref, dp_ref, accv, acck)
-        attend_block(0, True, head, *refs)
-
-        @pl.loop(1, SEQ // QB)
+    def gradients_of(head, slot):
+        refs = (head, slot, qb, vb, gt, et, p_ref, l_ref, o_ref, accv, acck)
+        gradient_block(0, True, *refs)
+
+        @pl.loop(1, SEQ // GB)
         def _(block):
-            attend_block(pl.multiple_of(block * QB, QB), False, head, *refs)
-
-        entry_both = jnp.concatenate(split(et[...]), 0)
-        value_part = dot(entry_both, accv[...].astype(BF16))
-        key_part = dot(entry_both, acck[:, :HD].astype(BF16))
-        query_part = dot_split(acck[:, HD:], kb_ref[head], TN)
+            gradient_block(pl.multiple_of(block * GB, GB), False, *refs)
+
+        entry = et[...]
+        value_part = dot(entry, accv[...].astype(BF16))
+        key_part = dot(entry, acck[:, :HD].astype(BF16))
+        query_part = dot(acck[:, HD:].astype(BF16), kb_ref[head], TN)
+        query_part = query_part[:RIN] + query_part[RIN:]
         columns = pl.ds(pl.multiple_of(head * HD, HD), HD)
         sketch = None
         for kind, piece in enumerate((query_part, key_part, value_part)):
-            term = dot_split(piece[:RIN] + piece[RIN:], fv[kind, columns, :])
+            term = dot_split(piece, fv[kind, columns, :])
             sketch = term if sketch is None else sketch + term
         part[1] += sketch * NORM
 
+    @pl.loop(0, 2)
+    def _(head):
+        gradients_of(head, head)
+
+    wait_head(2)
+    softmax_of(2, 0)
+    gradients_of(2, 0)
+
     @pl.loop(1, PEERS)
     def _(step):
-        peer = (s + step) % PEERS
+        peer = peer_of(step)
         rows = pl.ds(pl.multiple_of(peer * 8, 8), 8)
         remote(part.at[:, rows, :], gather.at[s], r_send, r_recv, (f, peer)).start()
 
@@ -366,6 +433,9 @@
 
 
 def local(*operands):
+    operands = list(operands)
+    for place in (9, 11):
+        operands[place] = operands[place].T
     dma = pltpu.SemaphoreType.DMA
     any_spec = pl.BlockSpec(memory_space=pl.ANY)
     in_specs = [any_spec] * 13
@@ -380,20 +450,22 @@
             pltpu.VMEM((HPD, SEQ, HD), BF16),
             pltpu.VMEM((HPD, SEQ, HD), BF16),
             pltpu.VMEM((HPD * HD, SEQ), BF16),
-            pltpu.VMEM((RIN, SEQ), F32),
+            pltpu.VMEM((RIN, SEQ), BF16),
             pltpu.VMEM((4, TOK, D), BF16),
             pltpu.VMEM((RINGS, WROWS, D), BF16),
             pltpu.VMEM((RINGS, 4, WROWS, TOK), BF16),
             pltpu.VMEM((TOK, D), BF16),
             pltpu.VMEM((TOK, D), BF16),
             pltpu.VMEM((64, D), F32),
-            pltpu.VMEM((D, RIN), BF16),
-            pltpu.VMEM((D, RIN), BF16),
+            pltpu.VMEM((RIN, D), BF16),
+            pltpu.VMEM((RIN, D), BF16),
             pltpu.VMEM((D, ROUT), BF16),
             pltpu.VMEM((3, HPD * HD, ROUT), BF16),
-            pltpu.VMEM((SEQ, QB), F32),
-            pltpu.VMEM((SEQ, QB), BF16),
-            pltpu.VMEM((SEQ, QB), F32),
+            pltpu.VMEM((2, SEQ, SB), F32),
+            pltpu.VMEM((2, SEQ, SEQ), BF16),
+            pltpu.VMEM((2, SEQ), F32),
+            pltpu.VMEM((2, HD, SEQ), F32),
+            pltpu.VMEM((HD, SEQ), BF16),
             pltpu.VMEM((SEQ, HD), F32),
             pltpu.VMEM((SEQ, 2 * HD), F32),
             pltpu.VMEM((2, RIN, ROUT), F32),

time: 160 us -> 114 us (0.71)
  the two profiles are of different devices: /device:TPU:1 before, /device:TPU:8 now
where the time goes in v2:
time: 114 us
  Pallas kernels  112 us (98%)
  local copies, waits for them, and re-layouts  1.3 us (1%)
    pallas_call x1, Pallas kernels, local(): pl.pallas_call(kernel, out_shape=jax.ShapeDtypeStruct((1, 2, RIN * ROUT /...  112 us

profile of v2, /device:TPU:8, one launch (start us, length us, event | category | flops | bytes accessed | tf_op | source)
XLA Modules:
  0.0 113.8 jit_solution(3871276364913123212)
XLA Ops:
  0.7 111.9 %shard_map.127 = f32[1,2,1024]{2,1,0:T(2,128)} custom-call(bf16[1,256,3072]{2,1,0:T(8,128)(2,1)} %xn.1, bf16[1,256,3072]{2,1,0:T(8,128)(2,1)} %qh.1, bf16[1,256,3072]{2,1,0:T(8,128)(2,1)} %kh.1, bf16[1,256,3072]{2,1,0:T(8,128)(2,1)} %vh.1, bf16[1,256,3072]{2,1,0:T(8,128)(2,1)} %ao.1, bf16[1,256,3072]{2,1,0:T(8,128)(2,1)} %og.1, bf16[192,3072]{1,0:T(8,128)(2,1)} %wh.1, ...), custom_call_target="tpu_custom_call" | custom-call | flops 25999998976 | bytes 16777216 | tf_op jit(solution)/shard_map/pallas_call | solution.py:443
  112.5 1.3 %copy.16 = f32[1,2,1024]{2,1,0:T(2,128)} copy(f32[1,2,1024]{2,1,0:T(2,128)} %shard_map.127) | data formatting | bytes 16384

commit v3 on v2

--- a/solution.py
+++ b/solution.py
@@ -54,8 +54,20 @@
     return reduce(values.reshape(rows // 8, 8, columns), axis=0)
 
 
-def softmax_head(head, slot, qb, kb_ref, vb, s_ref, p_ref, l_ref, o_ref, vt):
-    vt[...] = vb[head].T
+def values_of_head(head, slot, vb, et, p_ref, o_ref, vt):
+    vt[:HD] = vb[head].T
+    vt[HD:] = et[...]
+
+    @pl.loop(0, SEQ // 512)
+    def _(block):
+        columns = pl.ds(pl.multiple_of(block * 512, 512), 512)
+        o_ref[slot, :, columns] = dot(vt[...], p_ref[slot, :, columns])
+
+
+def softmax_head(head, slot, with_values, qb, kb_ref, vb, et, s_ref, p_ref, l_ref, o_ref, vt):
+    if with_values:
+        vt[:HD] = vb[head].T
+        vt[HD:] = et[...]
 
     def queries(start):
         wide = qb[head, pl.ds(start, SB), :].astype(F32).T
@@ -75,14 +87,16 @@
         part = fold(probs, jnp.sum)
         probs = probs.astype(BF16)
         p_ref[slot, rows, columns] = probs
-        piece = dot(vt[:, rows], probs)
-        if total is None:
-            return part, piece
-        return total + part, mixed + piece
+        total = part if total is None else total + part
+        if with_values:
+            piece = dot(vt[:, rows], probs)
+            mixed = piece if mixed is None else mixed + piece
+        return total, mixed
 
     def finish(columns, total, mixed):
         l_ref[pl.ds(slot, 1), columns] = jnp.sum(total, axis=0, keepdims=True)
-        o_ref[slot, :, columns] = mixed
+        if with_values:
+            o_ref[slot, :, columns] = mixed
 
     def highest(top):
         return jnp.max(top, axis=0, keepdims=True)
@@ -119,8 +133,12 @@
     inverse = 1.0 / l_ref[pl.ds(slot, 1), columns]
     grads = gt[pl.ds(pl.multiple_of(head * HD, HD), HD), columns]
     wide = grads.astype(F32)
-    centre = jnp.sum(wide * o_ref[slot, :, columns], axis=0, keepdims=True) * inverse
-    grads_scaled = (wide * inverse).astype(BF16)
+    centre = jnp.sum(wide * o_ref[slot, :HD, columns], axis=0, keepdims=True) * inverse
+    add_v = dot_split(o_ref[slot, HD:, columns] * inverse, grads, NT)
+    if first:
+        accv[...] = add_v
+    else:
+        accv[...] += add_v
     inverse = inverse * SCALE
     entry_high, entry_low = split(et[:, columns].astype(F32) * inverse)
     q_scaled = (qb[head, columns, :].astype(F32).T * inverse).astype(BF16)
@@ -130,13 +148,10 @@
         probs = p_ref[slot, rows, columns]
         prob_grad = dot(vb[head, rows, :], grads)
         score_grad = (probs.astype(F32) * (prob_grad - centre)).astype(BF16)
-        add_v = dot(probs, grads_scaled, NT)
         add_k = dot(score_grad, q_entry, NT)
         if first:
-            accv[rows, :] = add_v
             acck[rows, :] = add_k
         else:
-            accv[rows, :] += add_v
             acck[rows, :] += add_k
 
 
@@ -156,6 +171,11 @@
     lo = s // 4
     zz = s % 4
     s_across = (1 - lo) * 4 + zz
+
+    def heads_of(lo, z):
+        return (2 * z + (lo + z) % 2) * HPD * HD
+
+    mine = heads_of(lo, zz)
     mate = (f + 1 - 2 * core, s)
     across_f = y * 4 + (1 - hi) * 2 + core
     across = (across_f, s_across)
@@ -164,8 +184,7 @@
 
     barrier = pltpu.get_barrier_semaphore()
 
-    @pl.loop(1, 32)
-    def _(step):
+    for step in range(1, 32):
         target = (y * 4 + (f % 4 + step // 8) % 4, (s + step) % 8)
         pl.semaphore_signal(barrier, inc=1, device_id=target, device_id_type=MESH)
 
@@ -182,14 +201,16 @@
 
     load_og = load(og.at[0], sg.at[0])
     load_gate = load(gates, gv)
-    load_w = load(wh, wb.at[y])
+    load_w = load(wh, wb.at[0])
     load_xn = load(xn.at[0], xv)
     load_ef = load(ef, efv)
     load_ao = load(ao.at[0], av)
     load_mf = load(mixf, mfv)
     load_rf = load(resf, rfv)
     load_f = [
-        load(mergedf.at[pl.ds(pl.multiple_of(kind * D + s * 384, 128), 384), :], fv.at[kind])
+        load(
+            mergedf.at[pl.ds(pl.multiple_of(kind * D + mine, HD), HPD * HD), :], fv.at[kind]
+        )
         for kind in range(3)
     ]
 
@@ -198,7 +219,7 @@
     here = pl.ds(pl.multiple_of(s * TOK, TOK), TOK)
     for head in range(HPD):
         for which in range(3):
-            columns = pl.ds(pl.multiple_of(s * 384 + head * HD, HD), HD)
+            columns = pl.ds(pl.multiple_of(mine + head * HD, HD), HD)
             pltpu.make_async_copy(
                 sources[which].at[0, :, columns],
                 targets[which].at[head, here, :],
@@ -216,22 +237,25 @@
     first_half = pl.ds(0, HALF)
     second_half = pl.ds(HALF, HALF)
     w_copies = [
-        remote(wh.at[first_half], wb.at[y, first_half], w_send.at[0], w_recv.at[0], up),
-        remote(wh.at[second_half], wb.at[y, second_half], w_send.at[1], w_recv.at[1], down),
-        remote(wh.at[second_half], wb.at[y, second_half], w_send.at[2], w_recv.at[2], up),
-        remote(wh.at[first_half], wb.at[y, first_half], w_send.at[3], w_recv.at[3], down),
+        remote(wh.at[first_half], wb.at[2, first_half], w_send.at[0], w_recv.at[0], up),
+        remote(wh.at[second_half], wb.at[1, second_half], w_send.at[1], w_recv.at[1], down),
+        remote(wh.at[second_half], wb.at[2, second_half], w_send.at[2], w_recv.at[2], up),
+        remote(wh.at[first_half], wb.at[1, first_half], w_send.at[3], w_recv.at[3], down),
     ]
     for copy in w_copies:
         copy.start()
     def peer_of(step):
         return ((lo + step // 4) % 2) * 4 + (zz + step) % 4
 
-    def send_head(head):
+    def heads_of_peer(step):
+        return heads_of((lo + step // 4) % 2, (zz + step) % 4)
+
+    def send_head(head, kinds=(0, 1, 2)):
         @pl.loop(1, PEERS)
         def _(step):
             peer = peer_of(step)
-            columns = pl.ds(pl.multiple_of(peer * 384 + head * HD, HD), HD)
-            for which in range(3):
+            columns = pl.ds(pl.multiple_of(heads_of_peer(step) + head * HD, HD), HD)
+            for which in kinds:
                 remote(
                     sources[which].at[0, :, columns],
                     targets[which].at[head, here, :],
@@ -254,8 +278,6 @@
     sg_mate = remote(sg.at[0], sg.at[1], sg_send.at[0], sg_recv.at[0], mate)
     sg_mate.start()
 
-    send_head(1)
-
     load_xn.wait()
     load_ef.wait()
     et[:, here] = dot(efv[...], xv[...], NT).astype(BF16)
@@ -264,6 +286,8 @@
     def _(step):
         peer = peer_of(step)
         remote(et.at[:, here], et.at[:, here], e_send, e_recv, (f, peer)).start()
+
+    send_head(1)
 
     load_ao.wait()
     load_mf.wait()
@@ -272,95 +296,89 @@
     mixed_right = dot(sg[0], rfv[...])
     part[0] = dot(mixed_left, mixed_right, precision=lax.Precision.HIGHEST) * NORM
 
-    def g_copies(chunk, image):
+    def g_copies(place, image):
+        chunk = (y + (0, 1, 3, 2)[place]) % 4
         token_block = s if image < 2 else s_across
         image_f = (f, mate[0], across_f, across_f + 1 - 2 * core)[image]
-        peer = 2 * chunk + hi
+        peer = ((chunk + hi) % 2) * 4 + chunk
         columns = pl.ds(pl.multiple_of(token_block * TOK, TOK), TOK)
         target = gt.at[pl.ds(pl.multiple_of(core * WROWS, WROWS), WROWS), columns]
-        slot = chunk * 4 + image
-        far = remote(
-            gst.at[chunk, image], target, g_send.at[slot], g_recv, (image_f, peer)
-        )
-        near = pltpu.make_async_copy(gst.at[chunk, image], target, g_recv)
+        source = gst.at[place, image]
+        far = remote(source, target, g_send.at[place * 4 + image], g_recv, (image_f, peer))
+        near = pltpu.make_async_copy(source, target, g_recv)
         return far, near, peer
 
-    def make_g(chunk, image):
-        gst[chunk, image] = dot(wb[chunk], sg[image], NT).astype(BF16)
-        far, near, peer = g_copies(chunk, image)
-        if image == 0:
-
-            @pl.when(peer == s)
-            def _():
-                near.start()
-
-            @pl.when(peer != s)
-            def _():
+    def make_g(first, last, image):
+        weights = wb[first:last].reshape((last - first) * WROWS, D)
+        grads = dot(weights, sg[image], NT).astype(BF16)
+        for place in range(first, last):
+            start = (place - first) * WROWS
+            gst[place, image] = grads[start : start + WROWS]
+            far, near, peer = g_copies(place, image)
+            if image == 0:
+
+                @pl.when(peer == s)
+                def _():
+                    near.start()
+
+                @pl.when(peer != s)
+                def _():
+                    far.start()
+            else:
                 far.start()
-        else:
-            far.start()
-
-    below, above, opposite = (y + 3) % 4, (y + 1) % 4, (y + 2) % 4
+
     load_w.wait()
-    make_g(y, 0)
+    make_g(0, 1, 0)
     sg_mate.wait_recv()
-    make_g(y, 1)
+    make_g(0, 1, 1)
     w_copies[0].wait_recv()
     relay_up = remote(
-        wb.at[below, first_half], wb.at[below, first_half], w_send.at[4], w_recv.at[4], up
+        wb.at[2, first_half], wb.at[3, first_half], w_send.at[4], w_recv.at[4], up
     )
     relay_up.start()
     w_copies[1].wait_recv()
     relay_down = remote(
-        wb.at[above, second_half], wb.at[above, second_half], w_send.at[5], w_recv.at[5], down
+        wb.at[1, second_half], wb.at[3, second_half], w_send.at[5], w_recv.at[5], down
     )
     relay_down.start()
 
-    def wait_head(head):
-        for which in range(3):
+    def wait_head(head, kinds=(0, 1, 2)):
+        for which in kinds:
             whole = targets[which].at[head]
             pltpu.make_async_copy(whole, whole, qkv_recv.at[which, head]).wait()
 
-    def softmax_of(head, slot):
-        softmax_head(head, slot, qb, kb_ref, vb, s_ref, p_ref, l_ref, o_ref, vt)
-
+    def softmax_of(head, slot, with_values=True):
+        softmax_head(
+            head, slot, with_values, qb, kb_ref, vb, et, s_ref, p_ref, l_ref, o_ref, vt
+        )
+
+    rest = pl.ds(0, SEQ - TOK)
+    pltpu.make_async_copy(et.at[:, rest], et.at[:, rest], e_recv).wait()
     wait_head(0)
     softmax_of(0, 0)
     w_copies[2].wait_recv()
     w_copies[3].wait_recv()
 
-    def two(image):
-        @pl.loop(0, 2)
-        def _(step):
-            make_g((y + 1 + 2 * step) % 4, image)
-
-    def four(image):
-        @pl.loop(0, 4)
-        def _(step):
-            make_g((y + step) % 4, image)
-
-    two(0)
-    two(1)
+
+    make_g(1, 3, 0)
+    make_g(1, 3, 1)
     sg_across.wait_recv()
     sg_pass = remote(sg.at[2], sg.at[3], sg_send.at[2], sg_recv.at[2], mate)
     sg_pass.start()
-    make_g(y, 2)
-    two(2)
+    make_g(0, 3, 2)
     relay_up.wait_recv()
     relay_down.wait_recv()
-    make_g(opposite, 0)
-    make_g(opposite, 1)
-    make_g(opposite, 2)
+    for image in range(3):
+        make_g(3, 4, image)
     sg_pass.wait_recv()
-    four(3)
-    send_head(2)
+    make_g(0, 4, 3)
+    send_head(2, (0, 1))
+    send_head(2, (2,))
     wait_head(1)
     softmax_of(1, 1)
 
     for copy in load_f:
         copy.wait()
-    rest = pl.ds(0, SEQ - TOK)
-    pltpu.make_async_copy(et.at[:, rest], et.at[:, rest], e_recv).wait()
     pltpu.make_async_copy(gt, gt, g_recv).wait()
     part[1] = jnp.zeros((RIN, ROUT), F32)
 
@@ -373,7 +391,7 @@
             gradient_block(pl.multiple_of(block * GB, GB), False, *refs)
 
         entry = et[...]
-        value_part = dot(entry, accv[...].astype(BF16))
+        value_part = accv[...]
         key_part = dot(entry, acck[:, :HD].astype(BF16))
         query_part = dot(acck[:, HD:].astype(BF16), kb_ref[head], TN)
         query_part = query_part[:RIN] + query_part[RIN:]
@@ -388,8 +406,10 @@
     def _(head):
         gradients_of(head, head)
 
-    wait_head(2)
-    softmax_of(2, 0)
+    wait_head(2, (0, 1))
+    softmax_of(2, 0, False)
+    wait_head(2, (2,))
+    values_of_head(2, 0, vb, et, p_ref, o_ref, vt)
     gradients_of(2, 0)
 
     @pl.loop(1, PEERS)
@@ -419,15 +439,10 @@
     for copy in (sg_mate, sg_across, sg_pass):
         copy.wait_send()
     for image in range(4):
-
-        @pl.loop(0, RINGS)
-        def _(chunk):
-            far, _, peer = g_copies(chunk, image)
+        for place in range(RINGS):
+            far, _, peer = g_copies(place, image)
             if image == 0:
-
-                @pl.when(peer != s)
-                def _():
-                    far.wait_send()
+                pl.when(peer != s)(far.wait_send)
             else:
                 far.wait_send()
 
@@ -464,9 +479,9 @@
             pltpu.VMEM((2, SEQ, SB), F32),
             pltpu.VMEM((2, SEQ, SEQ), BF16),
             pltpu.VMEM((2, SEQ), F32),
-            pltpu.VMEM((2, HD, SEQ), F32),
-            pltpu.VMEM((HD, SEQ), BF16),
-            pltpu.VMEM((SEQ, HD), F32),
+            pltpu.VMEM((2, HD + RIN, SEQ), F32),
+            pltpu.VMEM((HD + RIN, SEQ), BF16),
+            pltpu.VMEM((RIN, HD), F32),
             pltpu.VMEM((SEQ, 2 * HD), F32),
             pltpu.VMEM((2, RIN, ROUT), F32),
             pltpu.VMEM((PEERS, 2, 8, ROUT), F32),

time: 114 us -> 106 us (0.930)
  the two profiles are of different devices: /device:TPU:8 before, /device:TPU:1 now
where the time goes in v3:
time: 106 us
  Pallas kernels  104 us (98%)
  local copies, waits for them, and re-layouts  1.3 us (1%)
    pallas_call x1, Pallas kernels, local(): pl.pallas_call(kernel, out_shape=jax.ShapeDtypeStruct((1, 2, RIN * ROUT /...  104 us

profile of v3, /device:TPU:1, one launch (start us, length us, event | category | flops | bytes accessed | tf_op | source)
XLA Modules:
  0.0 105.7 jit_solution(13575641607461734366)
XLA Ops:
  0.7 103.7 %shard_map.127 = f32[1,2,1024]{2,1,0:T(2,128)} custom-call(bf16[1,256,3072]{2,1,0:T(8,128)(2,1)} %xn.1, bf16[1,256,3072]{2,1,0:T(8,128)(2,1)} %qh.1, bf16[1,256,3072]{2,1,0:T(8,128)(2,1)} %kh.1, bf16[1,256,3072]{2,1,0:T(8,128)(2,1)} %vh.1, bf16[1,256,3072]{2,1,0:T(8,128)(2,1)} %ao.1, bf16[1,256,3072]{2,1,0:T(8,128)(2,1)} %og.1, bf16[192,3072]{1,0:T(8,128)(2,1)} %wh.1, ...), custom_call_target="tpu_custom_call" | custom-call | flops 25999998976 | bytes 16777216 | tf_op jit(solution)/shard_map/pallas_call | solution.py:458
  104.4 1.3 %copy.16 = f32[1,2,1024]{2,1,0:T(2,128)} copy(f32[1,2,1024]{2,1,0:T(2,128)} %shard_map.127) | data formatting | bytes 16384

commit v4 on v3

--- a/solution.py
+++ b/solution.py
@@ -54,14 +54,20 @@
     return reduce(values.reshape(rows // 8, 8, columns), axis=0)
 
 
-def values_of_head(head, slot, vb, et, p_ref, o_ref, vt):
-    vt[:HD] = vb[head].T
-    vt[HD:] = et[...]
+def values_of_half(head, slot, base, first, vb, et, p_ref, o_ref, vt):
+    half = SEQ // 2
+    rows = pl.ds(base, half)
+    vt[:HD, :half] = vb[head, rows, :].T
+    vt[HD:, :half] = et[:, rows]
 
     @pl.loop(0, SEQ // 512)
     def _(block):
         columns = pl.ds(pl.multiple_of(block * 512, 512), 512)
-        o_ref[slot, :, columns] = dot(vt[...], p_ref[slot, :, columns])
+        mixed = dot(vt[:, :half], p_ref[slot, rows, columns])
+        if first:
+            o_ref[slot, :, columns] = mixed
+        else:
+            o_ref[slot, :, columns] += mixed
 
 
 def softmax_head(head, slot, with_values, qb, kb_ref, vb, et, s_ref, p_ref, l_ref, o_ref, vt):
@@ -160,7 +166,7 @@
     out,
     qb, kb_ref, vb, gt, et, sg, wb, gst, xv, av, gv, efv, mfv, rfv, fv,
     s_ref, p_ref, l_ref, o_ref, vt, accv, acck, part, gather,
-    load_sem, qkv_recv, qkv_send, w_recv, w_send, sg_recv, sg_send,
+    load_sem, qkv_recv, late_recv, qkv_send, w_recv, w_send, sg_recv, sg_send,
     g_recv, g_send, e_recv, e_send, r_recv, r_send,
 ):
     f = lax.axis_index("fsdp")
@@ -250,8 +256,8 @@
     def heads_of_peer(step):
         return heads_of((lo + step // 4) % 2, (zz + step) % 4)
 
-    def send_head(head, kinds=(0, 1, 2)):
-        @pl.loop(1, PEERS)
+    def send_head(head, kinds=(0, 1, 2), first=1, last=PEERS, late=False):
+        @pl.loop(first, last)
         def _(step):
             peer = peer_of(step)
             columns = pl.ds(pl.multiple_of(heads_of_peer(step) + head * HD, HD), HD)
@@ -260,7 +266,7 @@
                     sources[which].at[0, :, columns],
                     targets[which].at[head, here, :],
                     qkv_send.at[which, head],
-                    qkv_recv.at[which, head],
+                    late_recv if late else qkv_recv.at[which, head],
                     (f, peer),
                 ).start()
 
@@ -373,7 +379,8 @@
     sg_pass.wait_recv()
     make_g(0, 4, 3)
     send_head(2, (0, 1))
-    send_head(2, (2,))
+    send_head(2, (2,), 1, 4)
+    send_head(2, (2,), 4, PEERS, True)
     wait_head(1)
     softmax_of(1, 1)
 
@@ -408,8 +415,11 @@
 
     wait_head(2, (0, 1))
     softmax_of(2, 0, False)
-    wait_head(2, (2,))
-    values_of_head(2, 0, vb, et, p_ref, o_ref, vt)
+    halves = [pl.multiple_of(((lo + turn) % 2) * (SEQ // 2), SEQ // 2) for turn in range(2)]
+    for turn, arrived in enumerate((qkv_recv.at[2, 2], late_recv)):
+        part_values = vb.at[2, pl.ds(halves[turn], SEQ // 2)]
+        pltpu.make_async_copy(part_values, part_values, arrived).wait()
+        values_of_half(2, 0, halves[turn], turn == 0, vb, et, p_ref, o_ref, vt)
     gradients_of(2, 0)
 
     @pl.loop(1, PEERS)
@@ -487,6 +497,7 @@
             pltpu.VMEM((PEERS, 2, 8, ROUT), F32),
             dma((11,)),
             dma((3, HPD)),
+            dma,
             dma((3, HPD)),
             dma((6,)),
             dma((6,)),

time: 106 us -> 107 us (level)
  no operation moved by 1% of the time
where the time goes in v4:
time: 107 us; the launch traced here: 106 us
  Pallas kernels  105 us (98%)
  local copies, waits for them, and re-layouts  1.3 us (1%)
    pallas_call x1, Pallas kernels, local(): pl.pallas_call(kernel, out_shape=jax.ShapeDtypeStruct((1, 2, RIN * ROUT /...  105 us

profile of v4, /device:TPU:1, one launch (start us, length us, event | category | flops | bytes accessed | tf_op | source)
XLA Modules:
  0.0 106.5 jit_solution(13797166376824697894)
XLA Ops:
  0.7 104.5 %shard_map.127 = f32[1,2,1024]{2,1,0:T(2,128)} custom-call(bf16[1,256,3072]{2,1,0:T(8,128)(2,1)} %xn.1, bf16[1,256,3072]{2,1,0:T(8,128)(2,1)} %qh.1, bf16[1,256,3072]{2,1,0:T(8,128)(2,1)} %kh.1, bf16[1,256,3072]{2,1,0:T(8,128)(2,1)} %vh.1, bf16[1,256,3072]{2,1,0:T(8,128)(2,1)} %ao.1, bf16[1,256,3072]{2,1,0:T(8,128)(2,1)} %og.1, bf16[192,3072]{1,0:T(8,128)(2,1)} %wh.1, ...), custom_call_target="tpu_custom_call" | custom-call | flops 25999998976 | bytes 16777216 | tf_op jit(solution)/shard_map/pallas_call | solution.py:468
  105.2 1.3 %copy.16 = f32[1,2,1024]{2,1,0:T(2,128)} copy(f32[1,2,1024]{2,1,0:T(2,128)} %shard_map.127) | data formatting | bytes 16384

commit v5 on v3

--- a/solution.py
+++ b/solution.py
@@ -202,30 +202,10 @@
     load_og = load(og.at[0], sg.at[0])
     load_gate = load(gates, gv)
     load_w = load(wh, wb.at[0])
-    load_xn = load(xn.at[0], xv)
-    load_ef = load(ef, efv)
-    load_ao = load(ao.at[0], av)
-    load_mf = load(mixf, mfv)
-    load_rf = load(resf, rfv)
-    load_f = [
-        load(
-            mergedf.at[pl.ds(pl.multiple_of(kind * D + mine, HD), HPD * HD), :], fv.at[kind]
-        )
-        for kind in range(3)
-    ]
 
     sources = (qh, kh, vh)
     targets = (qb, kb_ref, vb)
     here = pl.ds(pl.multiple_of(s * TOK, TOK), TOK)
-    for head in range(HPD):
-        for which in range(3):
-            columns = pl.ds(pl.multiple_of(mine + head * HD, HD), HD)
-            pltpu.make_async_copy(
-                sources[which].at[0, :, columns],
-                targets[which].at[head, here, :],
-                qkv_recv.at[which, head],
-            ).start()
-
     pl.semaphore_wait(barrier, 33)
 
     def remote(source, target, send, recv, device):
@@ -277,6 +257,27 @@
     sg_across.start()
     sg_mate = remote(sg.at[0], sg.at[1], sg_send.at[0], sg_recv.at[0], mate)
     sg_mate.start()
+
+    load_xn = load(xn.at[0], xv)
+    load_ef = load(ef, efv)
+    load_ao = load(ao.at[0], av)
+    load_mf = load(mixf, mfv)
+    load_rf = load(resf, rfv)
+    load_f = [
+        load(
+            mergedf.at[pl.ds(pl.multiple_of(kind * D + mine, HD), HPD * HD), :], fv.at[kind]
+        )
+        for kind in range(3)
+    ]
+
+    for head in range(HPD):
+        for which in range(3):
+            columns = pl.ds(pl.multiple_of(mine + head * HD, HD), HD)
+            pltpu.make_async_copy(
+                sources[which].at[0, :, columns],
+                targets[which].at[head, here, :],
+                qkv_recv.at[which, head],
+            ).start()
 
     load_xn.wait()
     load_ef.wait()

time: 106 us -> 106 us (level)
  no operation moved by 1% of the time
where the time goes in v5:
time: 106 us
  Pallas kernels  104 us (98%)
  local copies, waits for them, and re-layouts  1.3 us (1%)
    pallas_call x1, Pallas kernels, local(): pl.pallas_call(kernel, out_shape=jax.ShapeDtypeStruct((1, 2, RIN * ROUT /...  104 us

profile of v5, /device:TPU:1, one launch (start us, length us, event | category | flops | bytes accessed | tf_op | source)
XLA Modules:
  0.0 105.7 jit_solution(14484451276955514927)
XLA Ops:
  0.7 103.8 %shard_map.127 = f32[1,2,1024]{2,1,0:T(2,128)} custom-call(bf16[1,256,3072]{2,1,0:T(8,128)(2,1)} %xn.1, bf16[1,256,3072]{2,1,0:T(8,128)(2,1)} %qh.1, bf16[1,256,3072]{2,1,0:T(8,128)(2,1)} %kh.1, bf16[1,256,3072]{2,1,0:T(8,128)(2,1)} %vh.1, bf16[1,256,3072]{2,1,0:T(8,128)(2,1)} %ao.1, bf16[1,256,3072]{2,1,0:T(8,128)(2,1)} %og.1, bf16[192,3072]{1,0:T(8,128)(2,1)} %wh.1, ...), custom_call_target="tpu_custom_call" | custom-call | flops 25999998976 | bytes 16777216 | tf_op jit(solution)/shard_map/pallas_call | solution.py:459
  104.4 1.3 %copy.16 = f32[1,2,1024]{2,1,0:T(2,128)} copy(f32[1,2,1024]{2,1,0:T(2,128)} %shard_map.127) | data formatting | bytes 16384
